TPU v7x, 256 devices: a whole 4x4x8 slice. The times are simulated.
256 devices in a mesh: gx: 32 (over x, z), gy: 8 (over y, core).
Axes of the slice: x: 4, y: 4, z: 8, core: 2. Of those that a mesh axis runs over, the one named last changes fastest.
Arguments:
- probes: bfloat16 [64, 256, 128, 128], P(None, 'gx', 'gy'), may hold values from -6 to 6
- permeability: float32 [256, 128, 128], P('gx', 'gy'), may hold values from 0.2 to 5
- absorption: float32 [256, 128, 128], P('gx', 'gy'), may hold values from 0.3 to 3
- sensitivity: float32 [256, 128, 128], P('gx', 'gy'), may hold values from -6 to 6
- observe_weight: float32 [256, 128, 128], P('gx', 'gy'), may hold values from 1 to 10
Outputs:
- q_basis: float32 [64, 256, 128, 128], P(None, 'gx', 'gy')
- r_factor: float32 [64, 64], replicated
All inputs are finite; a program needn't handle non-finite values.
Results may differ from a plain program's by a relative error of at most 0.0003.
Values sent between devices are 32-bit elements; how exact they have to be, the bound alone decides.
A program may use at most 128 MiB of HBM per device.

v0:
```python
import jax
import jax.numpy as jnp
from jax import lax
from jax.sharding import PartitionSpec as P

SWEEPS = 4


def padded_2(shard, sides, width):
    for axis, dim in sides:
        peers, length = (lax.axis_size(axis), shard.shape[dim])
        up = [(i, (i + 1) % peers) for i in range(peers - 1)]
        down = [(j, i) for i, j in up]
        last = lax.slice_in_dim(shard, length - width, length, axis=dim)
        first = lax.slice_in_dim(shard, 0, width, axis=dim)
        before = lax.ppermute(last, axis, up)
        after = lax.ppermute(first, axis, down)
        shard = jnp.concatenate([before, shard, after], axis=dim)
    return shard


def face_terms(kpad, absorption):
    center = kpad[1:-1, 1:-1]
    x_low = 0.5 * (center + kpad[:-2, 1:-1])
    x_high = 0.5 * (center + kpad[2:, 1:-1])
    y_low = 0.5 * (center + kpad[1:-1, :-2])
    y_high = 0.5 * (center + kpad[1:-1, 2:])
    zpad = jnp.pad(center, ((0, 0), (0, 0), (1, 1)))
    z_low = 0.5 * (center + zpad[:, :, :-2])
    z_high = 0.5 * (center + zpad[:, :, 2:])
    diag = absorption + x_low + x_high + y_low + y_high + z_low + z_high
    return ((x_low, x_high, y_low, y_high, z_low, z_high), diag)


def sweep(field, padded, rhs, coefs, diag):
    x_low, x_high, y_low, y_high, z_low, z_high = coefs
    zpad = jnp.pad(field, ((0, 0), (0, 0), (0, 0), (1, 1)))
    total = x_low * padded[:, :-2, 1:-1] + x_high * padded[:, 2:, 1:-1]
    total = total + y_low * padded[:, 1:-1, :-2] + y_high * padded[:, 1:-1, 2:]
    total = total + z_low * zpad[..., :-2] + z_high * zpad[..., 2:]
    return 0.2 * field + 0.8 * (rhs + total) / diag


def single_solve(rhs, coefs, diag):
    field = 0.8 * rhs / diag
    for step in range(SWEEPS - 1):
        padded = padded_2(field, (("gx", 1), ("gy", 2)), 1)
        field = sweep(field, padded, rhs, coefs, diag)
    return field


def lower_inverse(lower):
    width = lower.shape[0]
    identity = jnp.eye(width, dtype=jnp.float32)

    def row_step(index, inverse):
        row = lax.dynamic_slice_in_dim(lower, index, 1, 0)
        pivot = lax.dynamic_slice(lower, (index, index), (1, 1))
        unit = lax.dynamic_slice_in_dim(identity, index, 1, 0)
        partial_sum = jnp.dot(
            row, inverse, precision=lax.Precision.HIGHEST, preferred_element_type=jnp.float32
        )
        new_row = (unit - partial_sum) / pivot
        return lax.dynamic_update_slice_in_dim(inverse, new_row, index, 0)

    return lax.fori_loop(0, width, row_step, jnp.zeros((width, width), jnp.float32))


def body(probes, permeability, absorption, sensitivity, observe_weight):
    count, width_x, width_y, width_z = probes.shape
    total_cells = width_x * lax.axis_size("gx") * width_y * lax.axis_size("gy") * width_z
    source = sensitivity * probes.astype(jnp.float32)
    kpad = padded_2(permeability, (("gx", 0), ("gy", 1)), 1)
    coefs, diag = face_terms(kpad, absorption)
    forward = single_solve(source, coefs, diag)
    adjoint = single_solve(observe_weight * forward, coefs, diag)
    responses = (sensitivity * adjoint).reshape(count, -1)
    gram = jnp.dot(
        responses, responses.T, precision=lax.Precision.HIGHEST, preferred_element_type=jnp.float32
    ) / float(total_cells)
    summed = lax.psum(gram, ("gx", "gy"))
    r_factor = jnp.linalg.cholesky(summed).T
    inverse = lower_inverse(r_factor.T)
    q_basis = jnp.dot(
        inverse, responses, precision=lax.Precision.HIGHEST, preferred_element_type=jnp.float32
    )
    return (q_basis.reshape(count, width_x, width_y, width_z), r_factor)


def solution(mesh):
    return jax.shard_map(
        body,
        mesh=mesh,
        in_specs=(
            P(None, "gx", "gy", None),
            P("gx", "gy", None),
            P("gx", "gy", None),
            P("gx", "gy", None),
            P("gx", "gy", None),
        ),
        out_specs=(P(None, "gx", "gy", None), P()),
        check_vma=False,
    )
```

profile of v0, /device:TPU:1, one launch (start us, length us, event | category | flops | bytes accessed | tf_op | source)
XLA Modules:
  0.0 477.7 jit_solution(5736251679478385338)
XLA Ops:
  1.3 4.4 collective-permute-start
  7.9 2.4 collective-permute-done.1
  10.3 5.0 %collective-permute-start.2 = (f32[10,1,128]{2,1,0:T(1,128)S(1)}, f32[10,1,128]{2,1,0:T(1,128)S(1)}, u32[]{:S(2)}, u32[]{:S(2)}) collective-permute-start(f32[10,1,128]{2,1,0:T(1,128)S(1)} %get-tuple-element.132), channel_id=1, source_target_pairs={{0,1},{1,2},{2,3},{3,4},{4,5},{5,6},{6,7},{8,9},{9,10},{10,11},{11... | collective-permute-start | bytes 15368 | tf_op jit(solution)/shard_map/ppermute | solution.py:16
  17.3 3.0 collective-permute-done.3
  21.4 3.4 multiply_divide_fusion.1
  24.9 3.7 collective-permute-start.4
  29.9 9.0 %collective-permute-done.4 = f32[64,1,16,128]{3,0,2,1:T(8,128)S(1)} collective-permute-done((f32[64,1,16,128]{3,0,2,1:T(8,128)S(1)}, f32[64,1,16,128]{3,0,2,1:T(8,128)S(1)}, u32[]{:S(2)}, u32[]{:S(2)}) %collective-permute-start.4) | collective-permute-done | bytes 524320 | tf_op jit(solution)/shard_map/ppermute | solution.py:16
  38.9 5.1 %collective-permute-done.5 = f32[64,1,16,128]{3,0,2,1:T(8,128)S(1)} collective-permute-done((f32[64,1,16,128]{3,0,2,1:T(8,128)S(1)}, f32[64,1,16,128]{3,0,2,1:T(8,128)S(1)}, u32[]{:S(2)}, u32[]{:S(2)}) %collective-permute-start.5) | collective-permute-done | bytes 524320 | tf_op jit(solution)/shard_map/ppermute | solution.py:17
  44.1 3.9 collective-permute-start.6
  52.0 4.4 collective-permute-done.7
  56.4 7.8 %fusion.10 = f32[64,8,16,128]{3,0,2,1:T(8,128)S(1)} fusion(f32[64,8,16,128]{3,0,2,1:T(8,128)S(1)} %multiply_divide_fusion.1, f32[64,10,1,128]{3,0,2,1:T(8,128)S(1)} %collective-permute-done.7, f32[64,1,16,128]{3,0,2,1:T(8,128)S(1)} %collective-permute-done.5, f32[64,1,16,128]{3,0,2,1:T(8,128)S(1)} %collective-permute-done.4, ...), kind=kLoop, calls=%fused_computation.23 | loop fusion | flops 27262976 | bytes 12713984 | tf_op jit(solution)/shard_map/add | solution.py:41
  64.3 4.9 %collective-permute-start.8 = (f32[64,1,16,128]{3,0,2,1:T(8,128)S(1)}, f32[64,1,16,128]{3,0,2,1:T(8,128)S(1)}, u32[]{:S(2)}, u32[]{:S(2)}) collective-permute-start(f32[64,1,16,128]{3,0,2,1:T(8,128)S(1)} %get-tuple-element.127), channel_id=1, source_target_pairs={{0,8},{8,16},{16,24},{24,32},{32,40},{40,48},{48,56},{56,64},{64,7... | collective-permute-start | bytes 1572872 | tf_op jit(solution)/shard_map/ppermute | solution.py:16
  70.5 6.0 %collective-permute-done.8 = f32[64,1,16,128]{3,0,2,1:T(8,128)S(1)} collective-permute-done((f32[64,1,16,128]{3,0,2,1:T(8,128)S(1)}, f32[64,1,16,128]{3,0,2,1:T(8,128)S(1)}, u32[]{:S(2)}, u32[]{:S(2)}) %collective-permute-start.8) | collective-permute-done | bytes 524320 | tf_op jit(solution)/shard_map/ppermute | solution.py:16
  76.5 4.4 collective-permute-done.9
  81.0 6.2 %collective-permute-start.10 = (f32[64,10,1,128]{3,0,2,1:T(8,128)S(1)}, f32[64,10,1,128]{3,0,2,1:T(8,128)S(1)}, u32[]{:S(2)}, u32[]{:S(2)}) collective-permute-start(f32[64,10,1,128]{3,0,2,1:T(8,128)S(1)} %get-tuple-element.115), channel_id=1, source_target_pairs={{0,1},{1,2},{2,3},{3,4},{4,5},{5,6},{6,7},{8,9},{9,10},{10,11},{11... | collective-permute-start | bytes 983048 | tf_op jit(solution)/shard_map/ppermute | solution.py:16
  91.2 4.4 collective-permute-done.11
  95.6 7.8 %fusion.18 = f32[64,8,16,128]{3,0,2,1:T(8,128)S(1)} fusion(f32[64,8,16,128]{3,0,2,1:T(8,128)S(1)} %fusion.10, f32[64,10,1,128]{3,0,2,1:T(8,128)S(1)} %collective-permute-done.11, f32[64,1,16,128]{3,0,2,1:T(8,128)S(1)} %collective-permute-done.9, f32[64,1,16,128]{3,0,2,1:T(8,128)S(1)} %collective-permute-done.8, ...), kind=kLoop, calls=%fused_computation.31 | loop fusion | flops 27262976 | bytes 12713984 | tf_op jit(solution)/shard_map/add | solution.py:41
  103.5 4.0 collective-permute-start.12
  108.8 6.0 %collective-permute-done.12 = f32[64,1,16,128]{3,0,2,1:T(8,128)S(1)} collective-permute-done((f32[64,1,16,128]{3,0,2,1:T(8,128)S(1)}, f32[64,1,16,128]{3,0,2,1:T(8,128)S(1)}, u32[]{:S(2)}, u32[]{:S(2)}) %collective-permute-start.12) | collective-permute-done | bytes 524320 | tf_op jit(solution)/shard_map/ppermute | solution.py:16
  114.8 4.1 collective-permute-done.13
  119.0 6.7 %collective-permute-start.14 = (f32[64,10,1,128]{3,0,2,1:T(8,128)S(1)}, f32[64,10,1,128]{3,0,2,1:T(8,128)S(1)}, u32[]{:S(2)}, u32[]{:S(2)}) collective-permute-start(f32[64,10,1,128]{3,0,2,1:T(8,128)S(1)} %get-tuple-element.113), channel_id=1, source_target_pairs={{0,1},{1,2},{2,3},{3,4},{4,5},{5,6},{6,7},{8,9},{9,10},{10,11},{11... | collective-permute-start | bytes 983048 | tf_op jit(solution)/shard_map/ppermute | solution.py:16
  129.7 4.4 collective-permute-done.15
  134.1 7.9 %multiply_divide_fusion = (f32[64,8,16,128]{3,0,2,1:T(8,128)S(1)}, f32[64,8,16,128]{3,0,2,1:T(8,128)S(1)}) fusion(f32[8,16,128]{2,1,0:T(8,128)S(1)} %get-tuple-element.100, f32[8,16,128]{2,1,0:T(8,128)S(1)} %get-tuple-element.106, f32[64,8,16,128]{3,0,2,1:T(8,128)S(1)} %fusion.18, f32[8,16,128]{2,1,0:T(8,128)S(1)} %get-tuple-element.105, ...), kind=kLoop, calls=%fused_computation.158 | loop fusion | flops 30408704 | bytes 16973824 | tf_op jit(solution)/shard_map/div | solution.py:45
  145.5 6.0 %collective-permute-done.16 = f32[64,1,16,128]{3,0,2,1:T(8,128)S(1)} collective-permute-done((f32[64,1,16,128]{3,0,2,1:T(8,128)S(1)}, f32[64,1,16,128]{3,0,2,1:T(8,128)S(1)}, u32[]{:S(2)}, u32[]{:S(2)}) %collective-permute-start.16) | collective-permute-done | bytes 524320 | tf_op jit(solution)/shard_map/ppermute | solution.py:16
  151.5 4.1 collective-permute-done.17
  155.7 7.3 %collective-permute-start.18 = (f32[64,10,1,128]{3,0,2,1:T(8,128)S(1)}, f32[64,10,1,128]{3,0,2,1:T(8,128)S(1)}, u32[]{:S(2)}, u32[]{:S(2)}) collective-permute-start(f32[64,10,1,128]{3,0,2,1:T(8,128)S(1)} %get-tuple-element.111), channel_id=1, source_target_pairs={{0,1},{1,2},{2,3},{3,4},{4,5},{5,6},{6,7},{8,9},{9,10},{10,11},{11... | collective-permute-start | bytes 983048 | tf_op jit(solution)/shard_map/ppermute | solution.py:16
  163.0 2.4 collective-permute-start.19
  167.0 4.4 collective-permute-done.19
  171.4 13.2 %fusion.34 = f32[64,8,16,128]{3,0,2,1:T(8,128)S(1)} fusion(f32[64,8,16,128]{3,0,2,1:T(8,128)S(1)} %get-tuple-element.99, f32[64,8,16,128]{3,0,2,1:T(8,128)} %copy-done.4, f32[64,10,1,128]{3,0,2,1:T(8,128)S(1)} %collective-permute-done.19, f32[64,1,16,128]{3,0,2,1:T(8,128)S(1)} %collective-permute-done.17, f32[64,1,16,128]{3,0,2,1:T(8,128)S(1)} %collective-permute-done.16, ...), kind=kLoop, calls=%fused_computation.47 | loop fusion | flops 25165824 | bytes 14745600 | tf_op jit(solution)/shard_map/add | solution.py:41
  187.3 5.9 %collective-permute-done.20 = f32[64,1,16,128]{3,0,2,1:T(8,128)S(1)} collective-permute-done((f32[64,1,16,128]{3,0,2,1:T(8,128)S(1)}, f32[64,1,16,128]{3,0,2,1:T(8,128)S(1)}, u32[]{:S(2)}, u32[]{:S(2)}) %collective-permute-start.20) | collective-permute-done | bytes 524320 | tf_op jit(solution)/shard_map/ppermute | solution.py:16
  193.2 4.1 collective-permute-done.21
  197.4 6.9 %collective-permute-start.22 = (f32[64,10,1,128]{3,0,2,1:T(8,128)S(1)}, f32[64,10,1,128]{3,0,2,1:T(8,128)S(1)}, u32[]{:S(2)}, u32[]{:S(2)}) collective-permute-start(f32[64,10,1,128]{3,0,2,1:T(8,128)S(1)} %get-tuple-element.109), channel_id=1, source_target_pairs={{0,1},{1,2},{2,3},{3,4},{4,5},{5,6},{6,7},{8,9},{9,10},{10,11},{11... | collective-permute-start | bytes 983048 | tf_op jit(solution)/shard_map/ppermute | solution.py:16
  208.3 4.4 collective-permute-done.23
  212.7 13.2 %fusion.42 = f32[64,8,16,128]{3,0,2,1:T(8,128)S(1)} fusion(f32[64,8,16,128]{3,0,2,1:T(8,128)S(1)} %get-tuple-element.99, f32[64,8,16,128]{3,0,2,1:T(8,128)} %copy-done.3, f32[64,10,1,128]{3,0,2,1:T(8,128)S(1)} %collective-permute-done.23, f32[64,1,16,128]{3,0,2,1:T(8,128)S(1)} %collective-permute-done.21, f32[64,1,16,128]{3,0,2,1:T(8,128)S(1)} %collective-permute-done.20, ...), kind=kLoop, calls=%fused_computation.55 | loop fusion | flops 25165824 | bytes 14745600 | tf_op jit(solution)/shard_map/add | solution.py:41
  226.0 3.5 collective-permute-start.24
  230.8 6.0 %collective-permute-done.24 = f32[64,1,16,128]{3,0,2,1:T(8,128)S(1)} collective-permute-done((f32[64,1,16,128]{3,0,2,1:T(8,128)S(1)}, f32[64,1,16,128]{3,0,2,1:T(8,128)S(1)}, u32[]{:S(2)}, u32[]{:S(2)}) %collective-permute-start.24) | collective-permute-done | bytes 524320 | tf_op jit(solution)/shard_map/ppermute | solution.py:16
  236.8 4.1 collective-permute-done.25
  241.0 6.0 %collective-permute-start.26 = (f32[64,10,1,128]{3,0,2,1:T(8,128)S(1)}, f32[64,10,1,128]{3,0,2,1:T(8,128)S(1)}, u32[]{:S(2)}, u32[]{:S(2)}) collective-permute-start(f32[64,10,1,128]{3,0,2,1:T(8,128)S(1)} %get-tuple-element.107), channel_id=1, source_target_pairs={{0,1},{1,2},{2,3},{3,4},{4,5},{5,6},{6,7},{8,9},{9,10},{10,11},{11... | collective-permute-start | bytes 983048 | tf_op jit(solution)/shard_map/ppermute | solution.py:16
  251.0 4.4 collective-permute-done.27
  255.4 14.5 %fusion.97 = f32[64,8,16,128]{3,0,2,1:T(8,128)S(1)} fusion(f32[64,8,16,128]{3,0,2,1:T(8,128)} %copy-done, f32[64,8,16,128]{3,0,2,1:T(8,128)} %copy-done.2, f32[64,10,1,128]{3,0,2,1:T(8,128)S(1)} %collective-permute-done.27, f32[64,1,16,128]{3,0,2,1:T(8,128)S(1)} %collective-permute-done.25, f32[64,1,16,128]{3,0,2,1:T(8,128)S(1)} %collective-permute-done.24, ...), kind=kLoop, calls=%fused_computation.162 | loop fusion | flops 26214400 | bytes 14811136 | tf_op jit(solution)/shard_map/mul | solution.py:77
  271.9 3.4 fusion.98
  275.3 80.6 %psum.7 = f32[64,64]{0,1:T(8,128)S(1)} all-reduce(f32[64,64]{0,1:T(8,128)S(1)} %fusion.98), channel_id=1, replica_groups=mesh['gx'=32,'gy'=8] {'gx','gy'}, use_global_device_ids=true, to_apply=%region_0.1 | all-reduce | flops 4096 | bytes 32768 | tf_op jit(solution)/shard_map/psum | solution.py:81
  356.0 5.8 %cholesky.19 = f32[64,64]{1,0:T(8,128)S(1)} custom-call(f32[64,64]{1,0:T(8,128)S(1)} %fusion.112), custom_call_target="Cholesky" | custom-call | tf_op jit(solution)/shard_map/jit(cholesky)/cholesky | solution.py:82
  363.9 6.6 %copy.29 = f32[64,8,16,128]{3,2,1,0:T(8,128)} copy(f32[64,8,16,128]{3,0,2,1:T(8,128)} %copy-done.1) | data formatting | bytes 8388608 | tf_op jit(solution)/shard_map/mul | solution.py:77
  371.2 90.6 %while.13 = (s32[]{:T(128)}, f32[64,64]{1,0:T(8,128)S(1)}, f32[64,64]{1,0:T(8,128)S(1)}, f32[64,64]{1,0:T(8,128)S(1)}, s32[]{:T(128)}, /*index=5*/s32[]{:T(128)}) while((s32[]{:T(128)}, f32[64,64]{1,0:T(8,128)S(1)}, f32[64,64]{1,0:T(8,128)S(1)}, f32[64,64]{1,0:T(8,128)S(1)}, s32[]{:T(128)}, /*index=5*/s32[]{:T(128)}) %tuple.57), condition=%wide.region_4.5_spmd, body=%wide.region_3.4_spmd.sunk | while | flops 49282 | bytes 36181 | solution.py:66
  461.7 4.6 copy.46
  467.1 6.0 %fusion.94 = f32[64,8,16,128]{3,0,2,1:T(8,128)S(1)} fusion(f32[8,16,128,64]{2,1,0,3:T(8,128)S(1)} %bitcast.44, f32[64,64]{1,0:T(8,128)S(1)} %get-tuple-element.81), kind=kOutput, calls=%fused_computation.156 | convolution fusion | flops 805306368 | bytes 8404992 | tf_op jit(solution)/shard_map/dot_general | solution.py:84
  473.0 4.4 copy.31
  (259 shorter events, 134.3 us)
Async XLA Ops:
  1.3 5.7 %collective-permute-start = (f32[1,16,128]{2,1,0:T(8,128)S(1)}, f32[1,16,128]{2,1,0:T(8,128)S(1)}, u32[]{:S(2)}, u32[]{:S(2)}) collective-permute-start(f32[1,16,128]{2,1,0:T(8,128)S(1)} %get-tuple-element.134), channel_id=1, source_target_pairs={{0,8},{8,16},{16,24},{24,32},{32,40},{40,48},{48,56},{56,64},{64,7... | collective-permute-start | bytes 24584 | tf_op jit(solution)/shard_map/ppermute | solution.py:16
  5.7 4.6 collective-permute-start.1
  10.3 6.9 %collective-permute-start.2 = (f32[10,1,128]{2,1,0:T(1,128)S(1)}, f32[10,1,128]{2,1,0:T(1,128)S(1)}, u32[]{:S(2)}, u32[]{:S(2)}) collective-permute-start(f32[10,1,128]{2,1,0:T(1,128)S(1)} %get-tuple-element.132), channel_id=1, source_target_pairs={{0,1},{1,2},{2,3},{3,4},{4,5},{5,6},{6,7},{8,9},{9,10},{10,11},{11... | collective-permute-start | bytes 15368 | tf_op jit(solution)/shard_map/ppermute | solution.py:16
  15.3 4.9 %collective-permute-start.3 = (f32[10,1,128]{2,1,0:T(1,128)S(1)}, f32[10,1,128]{2,1,0:T(1,128)S(1)}, u32[]{:S(2)}, u32[]{:S(2)}) collective-permute-start(f32[10,1,128]{2,1,0:T(1,128)S(1)} %get-tuple-element.131), channel_id=1, source_target_pairs={{1,0},{2,1},{3,2},{4,3},{5,4},{6,5},{7,6},{9,8},{10,9},{11,10},{12... | collective-permute-start | bytes 15368 | tf_op jit(solution)/shard_map/ppermute | solution.py:17
  24.8 31.6 %copy-start.5 = (bf16[64,8,16,128]{3,2,1,0:T(8,128)(2,1)S(1)}, bf16[64,8,16,128]{3,2,1,0:T(8,128)(2,1)}, u32[]{:S(2)}) copy-start(bf16[64,8,16,128]{3,2,1,0:T(8,128)(2,1)} %param.7) | copy-start | bytes 6291460
  24.8 31.6 %copy-start.6 = (f32[8,16,128]{2,1,0:T(8,128)S(1)}, f32[8,16,128]{2,1,0:T(8,128)}, u32[]{:S(2)}) copy-start(f32[8,16,128]{2,1,0:T(8,128)} %param.10) | copy-start | bytes 196612
  24.9 14.0 %collective-permute-start.4 = (f32[64,1,16,128]{3,0,2,1:T(8,128)S(1)}, f32[64,1,16,128]{3,0,2,1:T(8,128)S(1)}, u32[]{:S(2)}, u32[]{:S(2)}) collective-permute-start(f32[64,1,16,128]{3,0,2,1:T(8,128)S(1)} %get-tuple-element.129), channel_id=1, source_target_pairs={{0,8},{8,16},{16,24},{24,32},{32,40},{40,48},{48,56},{56,64},{64,7... | collective-permute-start | bytes 1572872 | tf_op jit(solution)/shard_map/ppermute | solution.py:16
  28.6 15.4 %collective-permute-start.5 = (f32[64,1,16,128]{3,0,2,1:T(8,128)S(1)}, f32[64,1,16,128]{3,0,2,1:T(8,128)S(1)}, u32[]{:S(2)}, u32[]{:S(2)}) collective-permute-start(f32[64,1,16,128]{3,0,2,1:T(8,128)S(1)} %get-tuple-element.130), channel_id=1, source_target_pairs={{8,0},{16,8},{24,16},{32,24},{40,32},{48,40},{56,48},{64,56},{72,6... | collective-permute-start | bytes 1572872 | tf_op jit(solution)/shard_map/ppermute | solution.py:17
  44.1 7.9 %collective-permute-start.6 = (f32[64,10,1,128]{3,0,2,1:T(8,128)S(1)}, f32[64,10,1,128]{3,0,2,1:T(8,128)S(1)}, u32[]{:S(2)}, u32[]{:S(2)}) collective-permute-start(f32[64,10,1,128]{3,0,2,1:T(8,128)S(1)} %get-tuple-element.117), channel_id=1, source_target_pairs={{0,1},{1,2},{2,3},{3,4},{4,5},{5,6},{6,7},{8,9},{9,10},{10,11},{11... | collective-permute-start | bytes 983048 | tf_op jit(solution)/shard_map/ppermute | solution.py:16
  48.0 8.4 %collective-permute-start.7 = (f32[64,10,1,128]{3,0,2,1:T(8,128)S(1)}, f32[64,10,1,128]{3,0,2,1:T(8,128)S(1)}, u32[]{:S(2)}, u32[]{:S(2)}) collective-permute-start(f32[64,10,1,128]{3,0,2,1:T(8,128)S(1)} %get-tuple-element.118), channel_id=1, source_target_pairs={{1,0},{2,1},{3,2},{4,3},{5,4},{6,5},{7,6},{9,8},{10,9},{11,10},{12... | collective-permute-start | bytes 983048 | tf_op jit(solution)/shard_map/ppermute | solution.py:17
  64.3 12.2 %collective-permute-start.8 = (f32[64,1,16,128]{3,0,2,1:T(8,128)S(1)}, f32[64,1,16,128]{3,0,2,1:T(8,128)S(1)}, u32[]{:S(2)}, u32[]{:S(2)}) collective-permute-start(f32[64,1,16,128]{3,0,2,1:T(8,128)S(1)} %get-tuple-element.127), channel_id=1, source_target_pairs={{0,8},{8,16},{16,24},{24,32},{32,40},{40,48},{48,56},{56,64},{64,7... | collective-permute-start | bytes 1572872 | tf_op jit(solution)/shard_map/ppermute | solution.py:16
  69.2 11.7 %collective-permute-start.9 = (f32[64,1,16,128]{3,0,2,1:T(8,128)S(1)}, f32[64,1,16,128]{3,0,2,1:T(8,128)S(1)}, u32[]{:S(2)}, u32[]{:S(2)}) collective-permute-start(f32[64,1,16,128]{3,0,2,1:T(8,128)S(1)} %get-tuple-element.128), channel_id=1, source_target_pairs={{8,0},{16,8},{24,16},{32,24},{40,32},{48,40},{56,48},{64,56},{72,6... | collective-permute-start | bytes 1572872 | tf_op jit(solution)/shard_map/ppermute | solution.py:17
  81.0 10.2 %collective-permute-start.10 = (f32[64,10,1,128]{3,0,2,1:T(8,128)S(1)}, f32[64,10,1,128]{3,0,2,1:T(8,128)S(1)}, u32[]{:S(2)}, u32[]{:S(2)}) collective-permute-start(f32[64,10,1,128]{3,0,2,1:T(8,128)S(1)} %get-tuple-element.115), channel_id=1, source_target_pairs={{0,1},{1,2},{2,3},{3,4},{4,5},{5,6},{6,7},{8,9},{9,10},{10,11},{11... | collective-permute-start | bytes 983048 | tf_op jit(solution)/shard_map/ppermute | solution.py:16
  87.2 8.4 %collective-permute-start.11 = (f32[64,10,1,128]{3,0,2,1:T(8,128)S(1)}, f32[64,10,1,128]{3,0,2,1:T(8,128)S(1)}, u32[]{:S(2)}, u32[]{:S(2)}) collective-permute-start(f32[64,10,1,128]{3,0,2,1:T(8,128)S(1)} %get-tuple-element.116), channel_id=1, source_target_pairs={{1,0},{2,1},{3,2},{4,3},{5,4},{6,5},{7,6},{9,8},{10,9},{11,10},{12... | collective-permute-start | bytes 983048 | tf_op jit(solution)/shard_map/ppermute | solution.py:17
  103.4 30.7 %copy-start.7 = (f32[8,16,128]{2,1,0:T(8,128)S(1)}, f32[8,16,128]{2,1,0:T(8,128)}, u32[]{:S(2)}) copy-start(f32[8,16,128]{2,1,0:T(8,128)} %param.11) | copy-start | bytes 196612
  103.5 11.3 %collective-permute-start.12 = (f32[64,1,16,128]{3,0,2,1:T(8,128)S(1)}, f32[64,1,16,128]{3,0,2,1:T(8,128)S(1)}, u32[]{:S(2)}, u32[]{:S(2)}) collective-permute-start(f32[64,1,16,128]{3,0,2,1:T(8,128)S(1)} %get-tuple-element.125), channel_id=1, source_target_pairs={{0,8},{8,16},{16,24},{24,32},{32,40},{40,48},{48,56},{56,64},{64,7... | collective-permute-start | bytes 1572872 | tf_op jit(solution)/shard_map/ppermute | solution.py:16
  107.5 11.4 %collective-permute-start.13 = (f32[64,1,16,128]{3,0,2,1:T(8,128)S(1)}, f32[64,1,16,128]{3,0,2,1:T(8,128)S(1)}, u32[]{:S(2)}, u32[]{:S(2)}) collective-permute-start(f32[64,1,16,128]{3,0,2,1:T(8,128)S(1)} %get-tuple-element.126), channel_id=1, source_target_pairs={{8,0},{16,8},{24,16},{32,24},{40,32},{48,40},{56,48},{64,56},{72,6... | collective-permute-start | bytes 1572872 | tf_op jit(solution)/shard_map/ppermute | solution.py:17
  119.0 10.7 %collective-permute-start.14 = (f32[64,10,1,128]{3,0,2,1:T(8,128)S(1)}, f32[64,10,1,128]{3,0,2,1:T(8,128)S(1)}, u32[]{:S(2)}, u32[]{:S(2)}) collective-permute-start(f32[64,10,1,128]{3,0,2,1:T(8,128)S(1)} %get-tuple-element.113), channel_id=1, source_target_pairs={{0,1},{1,2},{2,3},{3,4},{4,5},{5,6},{6,7},{8,9},{9,10},{10,11},{11... | collective-permute-start | bytes 983048 | tf_op jit(solution)/shard_map/ppermute | solution.py:16
  125.7 8.4 %collective-permute-start.15 = (f32[64,10,1,128]{3,0,2,1:T(8,128)S(1)}, f32[64,10,1,128]{3,0,2,1:T(8,128)S(1)}, u32[]{:S(2)}, u32[]{:S(2)}) collective-permute-start(f32[64,10,1,128]{3,0,2,1:T(8,128)S(1)} %get-tuple-element.114), channel_id=1, source_target_pairs={{1,0},{2,1},{3,2},{4,3},{5,4},{6,5},{7,6},{9,8},{10,9},{11,10},{12... | collective-permute-start | bytes 983048 | tf_op jit(solution)/shard_map/ppermute | solution.py:17
  142.0 29.3 %copy-start.4 = (f32[64,8,16,128]{3,0,2,1:T(8,128)}, f32[64,8,16,128]{3,0,2,1:T(8,128)S(1)}, u32[]{:S(2)}) copy-start(f32[64,8,16,128]{3,0,2,1:T(8,128)S(1)} %get-tuple-element.98) | copy-start | bytes 12582916
  142.1 70.7 %copy-start = (f32[64,8,16,128]{3,0,2,1:T(8,128)}, f32[64,8,16,128]{3,0,2,1:T(8,128)S(1)}, u32[]{:S(2)}) copy-start(f32[64,8,16,128]{3,0,2,1:T(8,128)S(1)} %get-tuple-element.99) | copy-start | bytes 12582916
  142.1 9.4 %collective-permute-start.16 = (f32[64,1,16,128]{3,0,2,1:T(8,128)S(1)}, f32[64,1,16,128]{3,0,2,1:T(8,128)S(1)}, u32[]{:S(2)}, u32[]{:S(2)}) collective-permute-start(f32[64,1,16,128]{3,0,2,1:T(8,128)S(1)} %get-tuple-element.123), channel_id=1, source_target_pairs={{0,8},{8,16},{16,24},{24,32},{32,40},{40,48},{48,56},{56,64},{64,7... | collective-permute-start | bytes 1572872 | tf_op jit(solution)/shard_map/ppermute | solution.py:16
  144.2 11.4 %collective-permute-start.17 = (f32[64,1,16,128]{3,0,2,1:T(8,128)S(1)}, f32[64,1,16,128]{3,0,2,1:T(8,128)S(1)}, u32[]{:S(2)}, u32[]{:S(2)}) collective-permute-start(f32[64,1,16,128]{3,0,2,1:T(8,128)S(1)} %get-tuple-element.124), channel_id=1, source_target_pairs={{8,0},{16,8},{24,16},{32,24},{40,32},{48,40},{56,48},{64,56},{72,6... | collective-permute-start | bytes 1572872 | tf_op jit(solution)/shard_map/ppermute | solution.py:17
  155.7 11.3 %collective-permute-start.18 = (f32[64,10,1,128]{3,0,2,1:T(8,128)S(1)}, f32[64,10,1,128]{3,0,2,1:T(8,128)S(1)}, u32[]{:S(2)}, u32[]{:S(2)}) collective-permute-start(f32[64,10,1,128]{3,0,2,1:T(8,128)S(1)} %get-tuple-element.111), channel_id=1, source_target_pairs={{0,1},{1,2},{2,3},{3,4},{4,5},{5,6},{6,7},{8,9},{9,10},{10,11},{11... | collective-permute-start | bytes 983048 | tf_op jit(solution)/shard_map/ppermute | solution.py:16
  163.0 8.4 %collective-permute-start.19 = (f32[64,10,1,128]{3,0,2,1:T(8,128)S(1)}, f32[64,10,1,128]{3,0,2,1:T(8,128)S(1)}, u32[]{:S(2)}, u32[]{:S(2)}) collective-permute-start(f32[64,10,1,128]{3,0,2,1:T(8,128)S(1)} %get-tuple-element.112), channel_id=1, source_target_pairs={{1,0},{2,1},{3,2},{4,3},{5,4},{6,5},{7,6},{9,8},{10,9},{11,10},{12... | collective-permute-start | bytes 983048 | tf_op jit(solution)/shard_map/ppermute | solution.py:17
  184.6 23.7 %copy-start.3 = (f32[64,8,16,128]{3,0,2,1:T(8,128)}, f32[64,8,16,128]{3,0,2,1:T(8,128)S(1)}, u32[]{:S(2)}) copy-start(f32[64,8,16,128]{3,0,2,1:T(8,128)S(1)} %fusion.34) | copy-start | bytes 12582916
  184.7 8.5 %collective-permute-start.20 = (f32[64,1,16,128]{3,0,2,1:T(8,128)S(1)}, f32[64,1,16,128]{3,0,2,1:T(8,128)S(1)}, u32[]{:S(2)}, u32[]{:S(2)}) collective-permute-start(f32[64,1,16,128]{3,0,2,1:T(8,128)S(1)} %get-tuple-element.121), channel_id=1, source_target_pairs={{0,8},{8,16},{16,24},{24,32},{32,40},{40,48},{48,56},{56,64},{64,7... | collective-permute-start | bytes 1572872 | tf_op jit(solution)/shard_map/ppermute | solution.py:16
  186.0 11.3 %collective-permute-start.21 = (f32[64,1,16,128]{3,0,2,1:T(8,128)S(1)}, f32[64,1,16,128]{3,0,2,1:T(8,128)S(1)}, u32[]{:S(2)}, u32[]{:S(2)}) collective-permute-start(f32[64,1,16,128]{3,0,2,1:T(8,128)S(1)} %get-tuple-element.122), channel_id=1, source_target_pairs={{8,0},{16,8},{24,16},{32,24},{40,32},{48,40},{56,48},{64,56},{72,6... | collective-permute-start | bytes 1572872 | tf_op jit(solution)/shard_map/ppermute | solution.py:17
  197.4 10.9 %collective-permute-start.22 = (f32[64,10,1,128]{3,0,2,1:T(8,128)S(1)}, f32[64,10,1,128]{3,0,2,1:T(8,128)S(1)}, u32[]{:S(2)}, u32[]{:S(2)}) collective-permute-start(f32[64,10,1,128]{3,0,2,1:T(8,128)S(1)} %get-tuple-element.109), channel_id=1, source_target_pairs={{0,1},{1,2},{2,3},{3,4},{4,5},{5,6},{6,7},{8,9},{9,10},{10,11},{11... | collective-permute-start | bytes 983048 | tf_op jit(solution)/shard_map/ppermute | solution.py:16
  204.3 8.4 %collective-permute-start.23 = (f32[64,10,1,128]{3,0,2,1:T(8,128)S(1)}, f32[64,10,1,128]{3,0,2,1:T(8,128)S(1)}, u32[]{:S(2)}, u32[]{:S(2)}) collective-permute-start(f32[64,10,1,128]{3,0,2,1:T(8,128)S(1)} %get-tuple-element.110), channel_id=1, source_target_pairs={{1,0},{2,1},{3,2},{4,3},{5,4},{6,5},{7,6},{9,8},{10,9},{11,10},{12... | collective-permute-start | bytes 983048 | tf_op jit(solution)/shard_map/ppermute | solution.py:17
  225.9 15.0 %copy-start.2 = (f32[64,8,16,128]{3,0,2,1:T(8,128)}, f32[64,8,16,128]{3,0,2,1:T(8,128)S(1)}, u32[]{:S(2)}) copy-start(f32[64,8,16,128]{3,0,2,1:T(8,128)S(1)} %fusion.42) | copy-start | bytes 12582916
  226.0 10.8 %collective-permute-start.24 = (f32[64,1,16,128]{3,0,2,1:T(8,128)S(1)}, f32[64,1,16,128]{3,0,2,1:T(8,128)S(1)}, u32[]{:S(2)}, u32[]{:S(2)}) collective-permute-start(f32[64,1,16,128]{3,0,2,1:T(8,128)S(1)} %get-tuple-element.119), channel_id=1, source_target_pairs={{0,8},{8,16},{16,24},{24,32},{32,40},{40,48},{48,56},{56,64},{64,7... | collective-permute-start | bytes 1572872 | tf_op jit(solution)/shard_map/ppermute | solution.py:16
  229.5 11.4 %collective-permute-start.25 = (f32[64,1,16,128]{3,0,2,1:T(8,128)S(1)}, f32[64,1,16,128]{3,0,2,1:T(8,128)S(1)}, u32[]{:S(2)}, u32[]{:S(2)}) collective-permute-start(f32[64,1,16,128]{3,0,2,1:T(8,128)S(1)} %get-tuple-element.120), channel_id=1, source_target_pairs={{8,0},{16,8},{24,16},{32,24},{40,32},{48,40},{56,48},{64,56},{72,6... | collective-permute-start | bytes 1572872 | tf_op jit(solution)/shard_map/ppermute | solution.py:17
  241.0 10.0 %collective-permute-start.26 = (f32[64,10,1,128]{3,0,2,1:T(8,128)S(1)}, f32[64,10,1,128]{3,0,2,1:T(8,128)S(1)}, u32[]{:S(2)}, u32[]{:S(2)}) collective-permute-start(f32[64,10,1,128]{3,0,2,1:T(8,128)S(1)} %get-tuple-element.107), channel_id=1, source_target_pairs={{0,1},{1,2},{2,3},{3,4},{4,5},{5,6},{6,7},{8,9},{9,10},{10,11},{11... | collective-permute-start | bytes 983048 | tf_op jit(solution)/shard_map/ppermute | solution.py:16
  247.0 8.4 %collective-permute-start.27 = (f32[64,10,1,128]{3,0,2,1:T(8,128)S(1)}, f32[64,10,1,128]{3,0,2,1:T(8,128)S(1)}, u32[]{:S(2)}, u32[]{:S(2)}) collective-permute-start(f32[64,10,1,128]{3,0,2,1:T(8,128)S(1)} %get-tuple-element.108), channel_id=1, source_target_pairs={{1,0},{2,1},{3,2},{4,3},{5,4},{6,5},{7,6},{9,8},{10,9},{11,10},{12... | collective-permute-start | bytes 983048 | tf_op jit(solution)/shard_map/ppermute | solution.py:17
  269.9 2.0 copy-start.1
where the time goes:
time: 487 us; the launch traced here: 478 us
  waiting for transfers between devices  108 us (22%)
  starting transfers between devices  88.9 us (18%)
  blocking collectives  80.6 us (17%)
  other arithmetic  77.1 us (16%)
  local copies, waits for them, and re-layouts  60.6 us (12%)
  matrix products  59.3 us (12%)
    psum x1, blocking collectives, body(): summed = lax.psum(gram, ('gx', 'gy'))  80.6 us
    ppermute x14, starting transfers between devices, padded_2(): before = lax.ppermute(last, axis, up)  65.8 us
    ppermute x14, waiting for transfers between devices, padded_2(): after = lax.ppermute(first, axis, down)  57.8 us
    ppermute x14, waiting for transfers between devices, padded_2(): before = lax.ppermute(last, axis, up)  50.6 us
    dot_general x64, matrix products, row_step(): jnp.dot(row, inverse, precision=lax.Precision.HIGHEST, preferred_element_...  50 us
    add x4, other arithmetic, sweep(): return 0.2 * field + 0.8 * (rhs + total) / diag  42 us
    dynamic_slice x64, local copies, waits for them, and re-layouts, row_step(): pivot = lax.dynamic_slice(lower, (index, index), (1, 1))  37.6 us
    ppermute x14, starting transfers between devices, padded_2(): after = lax.ppermute(first, axis, down)  23.1 us
  transfers between devices with their start and end apart: 28, of which 26 were waited for; matrix products, arithmetic and copies ran while one was open for 0% of the time, Pallas kernels for 0%

commit v1 on v0

--- a/solution.py
+++ b/solution.py
@@ -78,7 +78,7 @@
     gram = jnp.dot(
         responses, responses.T, precision=lax.Precision.HIGHEST, preferred_element_type=jnp.float32
     ) / float(total_cells)
-    summed = lax.psum(gram, ("gx", "gy"))
+    summed = jnp.sum(lax.all_gather(gram, ("gx", "gy")), axis=0)
     r_factor = jnp.linalg.cholesky(summed).T
     inverse = lower_inverse(r_factor.T)
     q_basis = jnp.dot(

time: 487 us -> 527 us (1.082)
  waiting for transfers between devices: 108 us -> 218 us
  blocking collectives: 80.6 us -> 0 us
  between operations: 1.4 us -> 14.8 us
    all_gather x0 -> x1, waiting for transfers between devices: none -> 110 us  [body(): summed = jnp.sum(lax.all_gather(gram, ('gx', 'gy')), axis=0)]
    psum x1 -> x0, blocking collectives: 80.6 us -> none  [body(): summed = lax.psum(gram, ('gx', 'gy'))]
    mul x1, other arithmetic: 14.5 us -> 7.35 us  [body(): responses = (sensitivity * adjoint).reshape(count, -1)]
    unnamed x22 -> x16, local copies, waits for them, and re-layouts: 13.3 us -> 11.2 us
  transfers between devices with their start and end apart: 28 -> 29, of which waited for: 26 -> 27; matrix products, arithmetic and copies ran while one was open for 0% -> 2% of each run, Pallas kernels for 0% -> 0%
where the time goes in v1:
time: 527 us; the launch traced here: 518 us
  waiting for transfers between devices  218 us (41%)
  starting transfers between devices  88.8 us (17%)
  other arithmetic  74.1 us (14%)
  matrix products  64.3 us (12%)
  local copies, waits for them, and re-layouts  56.9 us (11%)
  between operations  14.8 us (3%)
    all_gather x1, waiting for transfers between devices, body(): summed = jnp.sum(lax.all_gather(gram, ('gx', 'gy')), axis=0)  110 us
    ppermute x14, starting transfers between devices, padded_2(): before = lax.ppermute(last, axis, up)  65.8 us
    ppermute x14, waiting for transfers between devices, padded_2(): after = lax.ppermute(first, axis, down)  57.8 us
    ppermute x14, waiting for transfers between devices, padded_2(): before = lax.ppermute(last, axis, up)  50.8 us
    dot_general x64, matrix products, row_step(): jnp.dot(row, inverse, precision=lax.Precision.HIGHEST, preferred_element_...  48.2 us
    add x4, other arithmetic, sweep(): return 0.2 * field + 0.8 * (rhs + total) / diag  42.1 us
    dynamic_slice x64, local copies, waits for them, and re-layouts, row_step(): pivot = lax.dynamic_slice(lower, (index, index), (1, 1))  38.1 us
    ppermute x14, starting transfers between devices, padded_2(): after = lax.ppermute(first, axis, down)  23 us
  transfers between devices with their start and end apart: 29, of which 27 were waited for; matrix products, arithmetic and copies ran while one was open for 2% of the time, Pallas kernels for 0%

profile of v1, /device:TPU:1, one launch (start us, length us, event | category | flops | bytes accessed | tf_op | source)
XLA Modules:
  0.0 518.3 jit_solution(5936495779950705464)
XLA Ops:
  7.9 4.4 collective-permute-start
  14.5 2.4 collective-permute-done.1
  16.9 5.0 collective-permute-start.2
  23.8 3.0 collective-permute-done.3
  28.0 3.4 multiply_divide_fusion.1
  31.5 3.7 collective-permute-start.4
  36.5 9.0 %collective-permute-done.4 = f32[64,1,16,128]{3,0,2,1:T(8,128)S(1)} collective-permute-done((f32[64,1,16,128]{3,0,2,1:T(8,128)S(1)}, f32[64,1,16,128]{3,0,2,1:T(8,128)S(1)}, u32[]{:S(2)}, u32[]{:S(2)}) %collective-permute-start.4) | collective-permute-done | bytes 524320 | tf_op jit(solution)/shard_map/ppermute | solution.py:16
  45.5 5.1 collective-permute-done.5
  50.7 3.9 collective-permute-start.6
  58.6 4.4 collective-permute-done.7
  63.0 7.8 %fusion.10 = f32[64,8,16,128]{3,0,2,1:T(8,128)S(1)} fusion(f32[64,8,16,128]{3,0,2,1:T(8,128)S(1)} %multiply_divide_fusion.1, f32[64,10,1,128]{3,0,2,1:T(8,128)S(1)} %collective-permute-done.7, f32[64,1,16,128]{3,0,2,1:T(8,128)S(1)} %collective-permute-done.5, f32[64,1,16,128]{3,0,2,1:T(8,128)S(1)} %collective-permute-done.4, ...), kind=kLoop, calls=%fused_computation.23 | loop fusion | flops 27262976 | bytes 12713984 | tf_op jit(solution)/shard_map/add | solution.py:41
  70.9 4.9 collective-permute-start.8
  77.1 6.0 %collective-permute-done.8 = f32[64,1,16,128]{3,0,2,1:T(8,128)S(1)} collective-permute-done((f32[64,1,16,128]{3,0,2,1:T(8,128)S(1)}, f32[64,1,16,128]{3,0,2,1:T(8,128)S(1)}, u32[]{:S(2)}, u32[]{:S(2)}) %collective-permute-start.8) | collective-permute-done | bytes 524320 | tf_op jit(solution)/shard_map/ppermute | solution.py:16
  83.1 4.4 collective-permute-done.9
  87.6 6.2 %collective-permute-start.10 = (f32[64,10,1,128]{3,0,2,1:T(8,128)S(1)}, f32[64,10,1,128]{3,0,2,1:T(8,128)S(1)}, u32[]{:S(2)}, u32[]{:S(2)}) collective-permute-start(f32[64,10,1,128]{3,0,2,1:T(8,128)S(1)} %get-tuple-element.115), channel_id=1, source_target_pairs={{0,1},{1,2},{2,3},{3,4},{4,5},{5,6},{6,7},{8,9},{9,10},{10,11},{11... | collective-permute-start | bytes 983048 | tf_op jit(solution)/shard_map/ppermute | solution.py:16
  97.8 4.4 collective-permute-done.11
  102.2 7.8 %fusion.18 = f32[64,8,16,128]{3,0,2,1:T(8,128)S(1)} fusion(f32[64,8,16,128]{3,0,2,1:T(8,128)S(1)} %fusion.10, f32[64,10,1,128]{3,0,2,1:T(8,128)S(1)} %collective-permute-done.11, f32[64,1,16,128]{3,0,2,1:T(8,128)S(1)} %collective-permute-done.9, f32[64,1,16,128]{3,0,2,1:T(8,128)S(1)} %collective-permute-done.8, ...), kind=kLoop, calls=%fused_computation.31 | loop fusion | flops 27262976 | bytes 12713984 | tf_op jit(solution)/shard_map/add | solution.py:41
  110.1 4.0 collective-permute-start.12
  115.4 6.0 %collective-permute-done.12 = f32[64,1,16,128]{3,0,2,1:T(8,128)S(1)} collective-permute-done((f32[64,1,16,128]{3,0,2,1:T(8,128)S(1)}, f32[64,1,16,128]{3,0,2,1:T(8,128)S(1)}, u32[]{:S(2)}, u32[]{:S(2)}) %collective-permute-start.12) | collective-permute-done | bytes 524320 | tf_op jit(solution)/shard_map/ppermute | solution.py:16
  121.4 4.1 collective-permute-done.13
  125.6 6.7 %collective-permute-start.14 = (f32[64,10,1,128]{3,0,2,1:T(8,128)S(1)}, f32[64,10,1,128]{3,0,2,1:T(8,128)S(1)}, u32[]{:S(2)}, u32[]{:S(2)}) collective-permute-start(f32[64,10,1,128]{3,0,2,1:T(8,128)S(1)} %get-tuple-element.113), channel_id=1, source_target_pairs={{0,1},{1,2},{2,3},{3,4},{4,5},{5,6},{6,7},{8,9},{9,10},{10,11},{11... | collective-permute-start | bytes 983048 | tf_op jit(solution)/shard_map/ppermute | solution.py:16
  136.3 4.4 collective-permute-done.15
  140.7 7.9 %multiply_divide_fusion = (f32[64,8,16,128]{3,0,2,1:T(8,128)S(1)}, f32[64,8,16,128]{3,0,2,1:T(8,128)S(1)}) fusion(f32[8,16,128]{2,1,0:T(8,128)S(1)} %get-tuple-element.100, f32[8,16,128]{2,1,0:T(8,128)S(1)} %get-tuple-element.106, f32[64,8,16,128]{3,0,2,1:T(8,128)S(1)} %fusion.18, f32[8,16,128]{2,1,0:T(8,128)S(1)} %get-tuple-element.105, ...), kind=kLoop, calls=%fused_computation.158 | loop fusion | flops 30408704 | bytes 16973824 | tf_op jit(solution)/shard_map/div | solution.py:45
  152.1 6.0 %collective-permute-done.16 = f32[64,1,16,128]{3,0,2,1:T(8,128)S(1)} collective-permute-done((f32[64,1,16,128]{3,0,2,1:T(8,128)S(1)}, f32[64,1,16,128]{3,0,2,1:T(8,128)S(1)}, u32[]{:S(2)}, u32[]{:S(2)}) %collective-permute-start.16) | collective-permute-done | bytes 524320 | tf_op jit(solution)/shard_map/ppermute | solution.py:16
  158.1 4.1 collective-permute-done.17
  162.3 7.3 %collective-permute-start.18 = (f32[64,10,1,128]{3,0,2,1:T(8,128)S(1)}, f32[64,10,1,128]{3,0,2,1:T(8,128)S(1)}, u32[]{:S(2)}, u32[]{:S(2)}) collective-permute-start(f32[64,10,1,128]{3,0,2,1:T(8,128)S(1)} %get-tuple-element.111), channel_id=1, source_target_pairs={{0,1},{1,2},{2,3},{3,4},{4,5},{5,6},{6,7},{8,9},{9,10},{10,11},{11... | collective-permute-start | bytes 983048 | tf_op jit(solution)/shard_map/ppermute | solution.py:16
  173.6 4.4 collective-permute-done.19
  178.0 13.2 %fusion.34 = f32[64,8,16,128]{3,0,2,1:T(8,128)S(1)} fusion(f32[64,8,16,128]{3,0,2,1:T(8,128)S(1)} %get-tuple-element.99, f32[64,8,16,128]{3,0,2,1:T(8,128)} %copy-done.1, f32[64,10,1,128]{3,0,2,1:T(8,128)S(1)} %collective-permute-done.19, f32[64,1,16,128]{3,0,2,1:T(8,128)S(1)} %collective-permute-done.17, f32[64,1,16,128]{3,0,2,1:T(8,128)S(1)} %collective-permute-done.16, ...), kind=kLoop, calls=%fused_computation.47 | loop fusion | flops 25165824 | bytes 14745600 | tf_op jit(solution)/shard_map/add | solution.py:41
  194.0 5.9 %collective-permute-done.20 = f32[64,1,16,128]{3,0,2,1:T(8,128)S(1)} collective-permute-done((f32[64,1,16,128]{3,0,2,1:T(8,128)S(1)}, f32[64,1,16,128]{3,0,2,1:T(8,128)S(1)}, u32[]{:S(2)}, u32[]{:S(2)}) %collective-permute-start.20) | collective-permute-done | bytes 524320 | tf_op jit(solution)/shard_map/ppermute | solution.py:16
  199.8 4.1 collective-permute-done.21
  204.0 6.9 %collective-permute-start.22 = (f32[64,10,1,128]{3,0,2,1:T(8,128)S(1)}, f32[64,10,1,128]{3,0,2,1:T(8,128)S(1)}, u32[]{:S(2)}, u32[]{:S(2)}) collective-permute-start(f32[64,10,1,128]{3,0,2,1:T(8,128)S(1)} %get-tuple-element.109), channel_id=1, source_target_pairs={{0,1},{1,2},{2,3},{3,4},{4,5},{5,6},{6,7},{8,9},{9,10},{10,11},{11... | collective-permute-start | bytes 983048 | tf_op jit(solution)/shard_map/ppermute | solution.py:16
  214.9 4.4 collective-permute-done.23
  219.3 13.2 %fusion.42 = f32[64,8,16,128]{3,0,2,1:T(8,128)S(1)} fusion(f32[64,8,16,128]{3,0,2,1:T(8,128)S(1)} %get-tuple-element.99, f32[64,8,16,128]{3,0,2,1:T(8,128)} %copy-done, f32[64,10,1,128]{3,0,2,1:T(8,128)S(1)} %collective-permute-done.23, f32[64,1,16,128]{3,0,2,1:T(8,128)S(1)} %collective-permute-done.21, f32[64,1,16,128]{3,0,2,1:T(8,128)S(1)} %collective-permute-done.20, ...), kind=kLoop, calls=%fused_computation.55 | loop fusion | flops 25165824 | bytes 14745600 | tf_op jit(solution)/shard_map/add | solution.py:41
  232.7 3.5 collective-permute-start.24
  237.4 6.0 %collective-permute-done.24 = f32[64,1,16,128]{3,0,2,1:T(8,128)S(1)} collective-permute-done((f32[64,1,16,128]{3,0,2,1:T(8,128)S(1)}, f32[64,1,16,128]{3,0,2,1:T(8,128)S(1)}, u32[]{:S(2)}, u32[]{:S(2)}) %collective-permute-start.24) | collective-permute-done | bytes 524320 | tf_op jit(solution)/shard_map/ppermute | solution.py:16
  243.4 4.1 collective-permute-done.25
  247.6 6.0 %collective-permute-start.26 = (f32[64,10,1,128]{3,0,2,1:T(8,128)S(1)}, f32[64,10,1,128]{3,0,2,1:T(8,128)S(1)}, u32[]{:S(2)}, u32[]{:S(2)}) collective-permute-start(f32[64,10,1,128]{3,0,2,1:T(8,128)S(1)} %get-tuple-element.107), channel_id=1, source_target_pairs={{0,1},{1,2},{2,3},{3,4},{4,5},{5,6},{6,7},{8,9},{9,10},{10,11},{11... | collective-permute-start | bytes 983048 | tf_op jit(solution)/shard_map/ppermute | solution.py:16
  257.7 4.4 collective-permute-done.27
  262.1 7.4 %fusion.97 = f32[64,8,16,128]{3,0,2,1:T(8,128)} fusion(f32[64,8,16,128]{3,0,2,1:T(8,128)S(1)} %get-tuple-element.99, f32[64,8,16,128]{3,0,2,1:T(8,128)S(1)} %fusion.42, f32[64,10,1,128]{3,0,2,1:T(8,128)S(1)} %collective-permute-done.27, f32[64,1,16,128]{3,0,2,1:T(8,128)S(1)} %collective-permute-done.25, f32[64,1,16,128]{3,0,2,1:T(8,128)S(1)} %collective-permute-done.24, ...), kind=kLoop, calls=%fused_computation.162 | loop fusion | flops 26214400 | bytes 14811136 | tf_op jit(solution)/shard_map/mul | solution.py:77
  269.4 7.6 %fusion.98 = f32[64,64]{1,0:T(8,128)} fusion(f32[64,8,16,128]{3,0,2,1:T(8,128)} %fusion.97), kind=kOutput, calls=%fused_computation.164 | convolution fusion | flops 805310464 | bytes 4210688 | tf_op jit(solution)/shard_map/dot_general | solution.py:78
  277.0 4.6 copy.25
  284.0 2.8 copy.32
  286.8 109.7 %all-gather.3.cloned.1.call-done = f32[16384,64]{1,0:T(8,128)} async-done(((f32[64,64]{1,0:T(8,128)}), f32[16384,64]{1,0:T(8,128)}) %all-gather.3.cloned.1.call-update) | async-done | bytes 4194320 | tf_op jit(solution)/shard_map/all_gather | solution.py:81
  396.5 4.0 reduce_sum.9
  400.6 5.8 %cholesky.19 = f32[64,64]{1,0:T(8,128)S(1)} custom-call(f32[64,64]{1,0:T(8,128)S(1)} %fusion.112), custom_call_target="Cholesky" | custom-call | tf_op jit(solution)/shard_map/jit(cholesky)/cholesky | solution.py:82
  409.1 89.0 %while.13 = (s32[]{:T(128)}, f32[64,64]{1,0:T(8,128)S(1)}, f32[64,64]{1,0:T(8,128)S(1)}, f32[64,64]{1,0:T(8,128)S(1)}, s32[]{:T(128)}, /*index=5*/s32[]{:T(128)}) while((s32[]{:T(128)}, f32[64,64]{1,0:T(8,128)S(1)}, f32[64,64]{1,0:T(8,128)S(1)}, f32[64,64]{1,0:T(8,128)S(1)}, s32[]{:T(128)}, /*index=5*/s32[]{:T(128)}) %tuple.57), condition=%wide.region_4.5_spmd, body=%wide.region_3.4_spmd.sunk | while | flops 49282 | bytes 36181 | solution.py:66
  498.2 8.6 %fusion.94 = f32[64,8,16,128]{3,0,2,1:T(8,128)S(1)} fusion(f32[8,16,128,64]{2,1,0,3:T(8,128)} %bitcast.46, f32[64,64]{1,0:T(8,128)S(1)} %get-tuple-element.81), kind=kOutput, calls=%fused_computation.156 | convolution fusion | flops 805306368 | bytes 8404992 | tf_op jit(solution)/shard_map/dot_general | solution.py:84
  506.8 4.4 copy.27
  (256 shorter events, 135.0 us)
Async XLA Ops:
  7.2 389.3 %all-gather.3.cloned.1.call-start = ((), (), s32[]{:S(2)}) async-start(), calls=%async_computation | async-start | bytes 8421376 | tf_op jit(solution)/shard_map/all_gather | solution.py:81
  7.9 5.7 %collective-permute-start = (f32[1,16,128]{2,1,0:T(8,128)S(1)}, f32[1,16,128]{2,1,0:T(8,128)S(1)}, u32[]{:S(2)}, u32[]{:S(2)}) collective-permute-start(f32[1,16,128]{2,1,0:T(8,128)S(1)} %get-tuple-element.134), channel_id=1, source_target_pairs={{0,8},{8,16},{16,24},{24,32},{32,40},{40,48},{48,56},{56,64},{64,7... | collective-permute-start | bytes 24584 | tf_op jit(solution)/shard_map/ppermute | solution.py:16
  12.3 4.6 collective-permute-start.1
  16.9 6.9 %collective-permute-start.2 = (f32[10,1,128]{2,1,0:T(1,128)S(1)}, f32[10,1,128]{2,1,0:T(1,128)S(1)}, u32[]{:S(2)}, u32[]{:S(2)}) collective-permute-start(f32[10,1,128]{2,1,0:T(1,128)S(1)} %get-tuple-element.132), channel_id=1, source_target_pairs={{0,1},{1,2},{2,3},{3,4},{4,5},{5,6},{6,7},{8,9},{9,10},{10,11},{11... | collective-permute-start | bytes 15368 | tf_op jit(solution)/shard_map/ppermute | solution.py:16
  21.9 4.9 collective-permute-start.3
  31.4 31.6 %copy-start.2 = (bf16[64,8,16,128]{3,2,1,0:T(8,128)(2,1)S(1)}, bf16[64,8,16,128]{3,2,1,0:T(8,128)(2,1)}, u32[]{:S(2)}) copy-start(bf16[64,8,16,128]{3,2,1,0:T(8,128)(2,1)} %param.7) | copy-start | bytes 6291460
  31.4 31.6 %copy-start.3 = (f32[8,16,128]{2,1,0:T(8,128)S(1)}, f32[8,16,128]{2,1,0:T(8,128)}, u32[]{:S(2)}) copy-start(f32[8,16,128]{2,1,0:T(8,128)} %param.10) | copy-start | bytes 196612
  31.5 14.0 %collective-permute-start.4 = (f32[64,1,16,128]{3,0,2,1:T(8,128)S(1)}, f32[64,1,16,128]{3,0,2,1:T(8,128)S(1)}, u32[]{:S(2)}, u32[]{:S(2)}) collective-permute-start(f32[64,1,16,128]{3,0,2,1:T(8,128)S(1)} %get-tuple-element.129), channel_id=1, source_target_pairs={{0,8},{8,16},{16,24},{24,32},{32,40},{40,48},{48,56},{56,64},{64,7... | collective-permute-start | bytes 1572872 | tf_op jit(solution)/shard_map/ppermute | solution.py:16
  35.2 15.4 %collective-permute-start.5 = (f32[64,1,16,128]{3,0,2,1:T(8,128)S(1)}, f32[64,1,16,128]{3,0,2,1:T(8,128)S(1)}, u32[]{:S(2)}, u32[]{:S(2)}) collective-permute-start(f32[64,1,16,128]{3,0,2,1:T(8,128)S(1)} %get-tuple-element.130), channel_id=1, source_target_pairs={{8,0},{16,8},{24,16},{32,24},{40,32},{48,40},{56,48},{64,56},{72,6... | collective-permute-start | bytes 1572872 | tf_op jit(solution)/shard_map/ppermute | solution.py:17
  50.7 7.9 %collective-permute-start.6 = (f32[64,10,1,128]{3,0,2,1:T(8,128)S(1)}, f32[64,10,1,128]{3,0,2,1:T(8,128)S(1)}, u32[]{:S(2)}, u32[]{:S(2)}) collective-permute-start(f32[64,10,1,128]{3,0,2,1:T(8,128)S(1)} %get-tuple-element.117), channel_id=1, source_target_pairs={{0,1},{1,2},{2,3},{3,4},{4,5},{5,6},{6,7},{8,9},{9,10},{10,11},{11... | collective-permute-start | bytes 983048 | tf_op jit(solution)/shard_map/ppermute | solution.py:16
  54.6 8.4 %collective-permute-start.7 = (f32[64,10,1,128]{3,0,2,1:T(8,128)S(1)}, f32[64,10,1,128]{3,0,2,1:T(8,128)S(1)}, u32[]{:S(2)}, u32[]{:S(2)}) collective-permute-start(f32[64,10,1,128]{3,0,2,1:T(8,128)S(1)} %get-tuple-element.118), channel_id=1, source_target_pairs={{1,0},{2,1},{3,2},{4,3},{5,4},{6,5},{7,6},{9,8},{10,9},{11,10},{12... | collective-permute-start | bytes 983048 | tf_op jit(solution)/shard_map/ppermute | solution.py:17
  70.9 12.2 %collective-permute-start.8 = (f32[64,1,16,128]{3,0,2,1:T(8,128)S(1)}, f32[64,1,16,128]{3,0,2,1:T(8,128)S(1)}, u32[]{:S(2)}, u32[]{:S(2)}) collective-permute-start(f32[64,1,16,128]{3,0,2,1:T(8,128)S(1)} %get-tuple-element.127), channel_id=1, source_target_pairs={{0,8},{8,16},{16,24},{24,32},{32,40},{40,48},{48,56},{56,64},{64,7... | collective-permute-start | bytes 1572872 | tf_op jit(solution)/shard_map/ppermute | solution.py:16
  75.8 11.7 %collective-permute-start.9 = (f32[64,1,16,128]{3,0,2,1:T(8,128)S(1)}, f32[64,1,16,128]{3,0,2,1:T(8,128)S(1)}, u32[]{:S(2)}, u32[]{:S(2)}) collective-permute-start(f32[64,1,16,128]{3,0,2,1:T(8,128)S(1)} %get-tuple-element.128), channel_id=1, source_target_pairs={{8,0},{16,8},{24,16},{32,24},{40,32},{48,40},{56,48},{64,56},{72,6... | collective-permute-start | bytes 1572872 | tf_op jit(solution)/shard_map/ppermute | solution.py:17
  87.6 10.2 %collective-permute-start.10 = (f32[64,10,1,128]{3,0,2,1:T(8,128)S(1)}, f32[64,10,1,128]{3,0,2,1:T(8,128)S(1)}, u32[]{:S(2)}, u32[]{:S(2)}) collective-permute-start(f32[64,10,1,128]{3,0,2,1:T(8,128)S(1)} %get-tuple-element.115), channel_id=1, source_target_pairs={{0,1},{1,2},{2,3},{3,4},{4,5},{5,6},{6,7},{8,9},{9,10},{10,11},{11... | collective-permute-start | bytes 983048 | tf_op jit(solution)/shard_map/ppermute | solution.py:16
  93.8 8.4 %collective-permute-start.11 = (f32[64,10,1,128]{3,0,2,1:T(8,128)S(1)}, f32[64,10,1,128]{3,0,2,1:T(8,128)S(1)}, u32[]{:S(2)}, u32[]{:S(2)}) collective-permute-start(f32[64,10,1,128]{3,0,2,1:T(8,128)S(1)} %get-tuple-element.116), channel_id=1, source_target_pairs={{1,0},{2,1},{3,2},{4,3},{5,4},{6,5},{7,6},{9,8},{10,9},{11,10},{12... | collective-permute-start | bytes 983048 | tf_op jit(solution)/shard_map/ppermute | solution.py:17
  110.0 30.7 %copy-start.4 = (f32[8,16,128]{2,1,0:T(8,128)S(1)}, f32[8,16,128]{2,1,0:T(8,128)}, u32[]{:S(2)}) copy-start(f32[8,16,128]{2,1,0:T(8,128)} %param.11) | copy-start | bytes 196612
  110.1 11.3 %collective-permute-start.12 = (f32[64,1,16,128]{3,0,2,1:T(8,128)S(1)}, f32[64,1,16,128]{3,0,2,1:T(8,128)S(1)}, u32[]{:S(2)}, u32[]{:S(2)}) collective-permute-start(f32[64,1,16,128]{3,0,2,1:T(8,128)S(1)} %get-tuple-element.125), channel_id=1, source_target_pairs={{0,8},{8,16},{16,24},{24,32},{32,40},{40,48},{48,56},{56,64},{64,7... | collective-permute-start | bytes 1572872 | tf_op jit(solution)/shard_map/ppermute | solution.py:16
  114.1 11.4 %collective-permute-start.13 = (f32[64,1,16,128]{3,0,2,1:T(8,128)S(1)}, f32[64,1,16,128]{3,0,2,1:T(8,128)S(1)}, u32[]{:S(2)}, u32[]{:S(2)}) collective-permute-start(f32[64,1,16,128]{3,0,2,1:T(8,128)S(1)} %get-tuple-element.126), channel_id=1, source_target_pairs={{8,0},{16,8},{24,16},{32,24},{40,32},{48,40},{56,48},{64,56},{72,6... | collective-permute-start | bytes 1572872 | tf_op jit(solution)/shard_map/ppermute | solution.py:17
  125.6 10.7 %collective-permute-start.14 = (f32[64,10,1,128]{3,0,2,1:T(8,128)S(1)}, f32[64,10,1,128]{3,0,2,1:T(8,128)S(1)}, u32[]{:S(2)}, u32[]{:S(2)}) collective-permute-start(f32[64,10,1,128]{3,0,2,1:T(8,128)S(1)} %get-tuple-element.113), channel_id=1, source_target_pairs={{0,1},{1,2},{2,3},{3,4},{4,5},{5,6},{6,7},{8,9},{9,10},{10,11},{11... | collective-permute-start | bytes 983048 | tf_op jit(solution)/shard_map/ppermute | solution.py:16
  132.3 8.4 %collective-permute-start.15 = (f32[64,10,1,128]{3,0,2,1:T(8,128)S(1)}, f32[64,10,1,128]{3,0,2,1:T(8,128)S(1)}, u32[]{:S(2)}, u32[]{:S(2)}) collective-permute-start(f32[64,10,1,128]{3,0,2,1:T(8,128)S(1)} %get-tuple-element.114), channel_id=1, source_target_pairs={{1,0},{2,1},{3,2},{4,3},{5,4},{6,5},{7,6},{9,8},{10,9},{11,10},{12... | collective-permute-start | bytes 983048 | tf_op jit(solution)/shard_map/ppermute | solution.py:17
  148.6 29.3 %copy-start.1 = (f32[64,8,16,128]{3,0,2,1:T(8,128)}, f32[64,8,16,128]{3,0,2,1:T(8,128)S(1)}, u32[]{:S(2)}) copy-start(f32[64,8,16,128]{3,0,2,1:T(8,128)S(1)} %get-tuple-element.98) | copy-start | bytes 12582916
  148.7 9.4 %collective-permute-start.16 = (f32[64,1,16,128]{3,0,2,1:T(8,128)S(1)}, f32[64,1,16,128]{3,0,2,1:T(8,128)S(1)}, u32[]{:S(2)}, u32[]{:S(2)}) collective-permute-start(f32[64,1,16,128]{3,0,2,1:T(8,128)S(1)} %get-tuple-element.123), channel_id=1, source_target_pairs={{0,8},{8,16},{16,24},{24,32},{32,40},{40,48},{48,56},{56,64},{64,7... | collective-permute-start | bytes 1572872 | tf_op jit(solution)/shard_map/ppermute | solution.py:16
  150.8 11.4 %collective-permute-start.17 = (f32[64,1,16,128]{3,0,2,1:T(8,128)S(1)}, f32[64,1,16,128]{3,0,2,1:T(8,128)S(1)}, u32[]{:S(2)}, u32[]{:S(2)}) collective-permute-start(f32[64,1,16,128]{3,0,2,1:T(8,128)S(1)} %get-tuple-element.124), channel_id=1, source_target_pairs={{8,0},{16,8},{24,16},{32,24},{40,32},{48,40},{56,48},{64,56},{72,6... | collective-permute-start | bytes 1572872 | tf_op jit(solution)/shard_map/ppermute | solution.py:17
  162.3 11.3 %collective-permute-start.18 = (f32[64,10,1,128]{3,0,2,1:T(8,128)S(1)}, f32[64,10,1,128]{3,0,2,1:T(8,128)S(1)}, u32[]{:S(2)}, u32[]{:S(2)}) collective-permute-start(f32[64,10,1,128]{3,0,2,1:T(8,128)S(1)} %get-tuple-element.111), channel_id=1, source_target_pairs={{0,1},{1,2},{2,3},{3,4},{4,5},{5,6},{6,7},{8,9},{9,10},{10,11},{11... | collective-permute-start | bytes 983048 | tf_op jit(solution)/shard_map/ppermute | solution.py:16
  169.6 8.4 %collective-permute-start.19 = (f32[64,10,1,128]{3,0,2,1:T(8,128)S(1)}, f32[64,10,1,128]{3,0,2,1:T(8,128)S(1)}, u32[]{:S(2)}, u32[]{:S(2)}) collective-permute-start(f32[64,10,1,128]{3,0,2,1:T(8,128)S(1)} %get-tuple-element.112), channel_id=1, source_target_pairs={{1,0},{2,1},{3,2},{4,3},{5,4},{6,5},{7,6},{9,8},{10,9},{11,10},{12... | collective-permute-start | bytes 983048 | tf_op jit(solution)/shard_map/ppermute | solution.py:17
  191.2 23.7 %copy-start = (f32[64,8,16,128]{3,0,2,1:T(8,128)}, f32[64,8,16,128]{3,0,2,1:T(8,128)S(1)}, u32[]{:S(2)}) copy-start(f32[64,8,16,128]{3,0,2,1:T(8,128)S(1)} %fusion.34) | copy-start | bytes 12582916
  191.3 8.5 %collective-permute-start.20 = (f32[64,1,16,128]{3,0,2,1:T(8,128)S(1)}, f32[64,1,16,128]{3,0,2,1:T(8,128)S(1)}, u32[]{:S(2)}, u32[]{:S(2)}) collective-permute-start(f32[64,1,16,128]{3,0,2,1:T(8,128)S(1)} %get-tuple-element.121), channel_id=1, source_target_pairs={{0,8},{8,16},{16,24},{24,32},{32,40},{40,48},{48,56},{56,64},{64,7... | collective-permute-start | bytes 1572872 | tf_op jit(solution)/shard_map/ppermute | solution.py:16
  192.7 11.3 %collective-permute-start.21 = (f32[64,1,16,128]{3,0,2,1:T(8,128)S(1)}, f32[64,1,16,128]{3,0,2,1:T(8,128)S(1)}, u32[]{:S(2)}, u32[]{:S(2)}) collective-permute-start(f32[64,1,16,128]{3,0,2,1:T(8,128)S(1)} %get-tuple-element.122), channel_id=1, source_target_pairs={{8,0},{16,8},{24,16},{32,24},{40,32},{48,40},{56,48},{64,56},{72,6... | collective-permute-start | bytes 1572872 | tf_op jit(solution)/shard_map/ppermute | solution.py:17
  204.0 10.9 %collective-permute-start.22 = (f32[64,10,1,128]{3,0,2,1:T(8,128)S(1)}, f32[64,10,1,128]{3,0,2,1:T(8,128)S(1)}, u32[]{:S(2)}, u32[]{:S(2)}) collective-permute-start(f32[64,10,1,128]{3,0,2,1:T(8,128)S(1)} %get-tuple-element.109), channel_id=1, source_target_pairs={{0,1},{1,2},{2,3},{3,4},{4,5},{5,6},{6,7},{8,9},{9,10},{10,11},{11... | collective-permute-start | bytes 983048 | tf_op jit(solution)/shard_map/ppermute | solution.py:16
  210.9 8.4 %collective-permute-start.23 = (f32[64,10,1,128]{3,0,2,1:T(8,128)S(1)}, f32[64,10,1,128]{3,0,2,1:T(8,128)S(1)}, u32[]{:S(2)}, u32[]{:S(2)}) collective-permute-start(f32[64,10,1,128]{3,0,2,1:T(8,128)S(1)} %get-tuple-element.110), channel_id=1, source_target_pairs={{1,0},{2,1},{3,2},{4,3},{5,4},{6,5},{7,6},{9,8},{10,9},{11,10},{12... | collective-permute-start | bytes 983048 | tf_op jit(solution)/shard_map/ppermute | solution.py:17
  232.7 10.8 %collective-permute-start.24 = (f32[64,1,16,128]{3,0,2,1:T(8,128)S(1)}, f32[64,1,16,128]{3,0,2,1:T(8,128)S(1)}, u32[]{:S(2)}, u32[]{:S(2)}) collective-permute-start(f32[64,1,16,128]{3,0,2,1:T(8,128)S(1)} %get-tuple-element.119), channel_id=1, source_target_pairs={{0,8},{8,16},{16,24},{24,32},{32,40},{40,48},{48,56},{56,64},{64,7... | collective-permute-start | bytes 1572872 | tf_op jit(solution)/shard_map/ppermute | solution.py:16
  236.1 11.4 %collective-permute-start.25 = (f32[64,1,16,128]{3,0,2,1:T(8,128)S(1)}, f32[64,1,16,128]{3,0,2,1:T(8,128)S(1)}, u32[]{:S(2)}, u32[]{:S(2)}) collective-permute-start(f32[64,1,16,128]{3,0,2,1:T(8,128)S(1)} %get-tuple-element.120), channel_id=1, source_target_pairs={{8,0},{16,8},{24,16},{32,24},{40,32},{48,40},{56,48},{64,56},{72,6... | collective-permute-start | bytes 1572872 | tf_op jit(solution)/shard_map/ppermute | solution.py:17
  247.6 10.0 %collective-permute-start.26 = (f32[64,10,1,128]{3,0,2,1:T(8,128)S(1)}, f32[64,10,1,128]{3,0,2,1:T(8,128)S(1)}, u32[]{:S(2)}, u32[]{:S(2)}) collective-permute-start(f32[64,10,1,128]{3,0,2,1:T(8,128)S(1)} %get-tuple-element.107), channel_id=1, source_target_pairs={{0,1},{1,2},{2,3},{3,4},{4,5},{5,6},{6,7},{8,9},{9,10},{10,11},{11... | collective-permute-start | bytes 983048 | tf_op jit(solution)/shard_map/ppermute | solution.py:16
  253.7 8.4 %collective-permute-start.27 = (f32[64,10,1,128]{3,0,2,1:T(8,128)S(1)}, f32[64,10,1,128]{3,0,2,1:T(8,128)S(1)}, u32[]{:S(2)}, u32[]{:S(2)}) collective-permute-start(f32[64,10,1,128]{3,0,2,1:T(8,128)S(1)} %get-tuple-element.108), channel_id=1, source_target_pairs={{1,0},{2,1},{3,2},{4,3},{5,4},{6,5},{7,6},{9,8},{10,9},{11,10},{12... | collective-permute-start | bytes 983048 | tf_op jit(solution)/shard_map/ppermute | solution.py:17
Sparse Core Ops, SparseCore 0:
  277.1 119.2 all-gather.2
